TPU v7x, 32 devices: a whole 2x2x4 slice. The times are simulated.
32 devices in a mesh: fsdp: 16 (over z, y, x), tp: 2 (over core).
Axes of the slice: x: 2, y: 2, z: 4, core: 2. Of those that a mesh axis runs over, the one named last changes fastest.
Arguments:
- hidden_in: bfloat16 [16384, 1024], P(('fsdp', 'tp')), may hold values from -6 to 6
- out_grad: bfloat16 [16384, 1024], P(('fsdp', 'tp')), may hold values from -6 to 6
- seq_lengths: int32 [16, 4], P('fsdp'), may hold values from 1 to 768, 1024 in all within a row
- norm_gain: float32 [1024], replicated, may hold values from 0.5 to 1.5
- w_z: bfloat16 [1024, 1536], P('fsdp', 'tp'), may hold values from -0.1875 to 0.1875
- w_x: bfloat16 [1024, 1536], P('fsdp', 'tp'), may hold values from -0.1875 to 0.1875
- w_bc: bfloat16 [1024, 256], P('fsdp'), may hold values from -0.1875 to 0.1875
- w_dt: bfloat16 [1024, 24], P('fsdp', 'tp'), may hold values from -0.1875 to 0.1875
- conv_x: float32 [4, 1536], replicated, may hold values from -3 to 3
- conv_bc: float32 [4, 256], replicated, may hold values from -3 to 3
- dt_bias: float32 [24], replicated, may hold values from -9 to -2
- a_log: float32 [24], replicated, may hold values from 0 to 2.5
- d_skip: float32 [24], replicated, may hold values from 0.5 to 2
- w_q: bfloat16 [1024, 512], P('fsdp', 'tp'), may hold values from -0.1875 to 0.1875
- key_matrix: bfloat16 [1024, 128], P('fsdp', 'tp'), may hold values from -0.1875 to 0.1875
- value_matrix: bfloat16 [1024, 128], P('fsdp', 'tp'), may hold values from -0.1875 to 0.1875
- w_o: bfloat16 [512, 1024], P('tp', 'fsdp'), may hold values from -1.5 to 1.5
- w_out: bfloat16 [1536, 1024], P('tp', 'fsdp'), may hold values from -0.15625 to 0.15625
- ff_gain: float32 [1024], replicated, may hold values from 0.5 to 1.5
- w_gate: bfloat16 [1024, 2048], P('fsdp', 'tp'), may hold values from -0.1875 to 0.1875
- w_up: bfloat16 [1024, 2048], P('fsdp', 'tp'), may hold values from -0.1875 to 0.1875
- w_down: bfloat16 [2048, 1024], P('tp', 'fsdp'), may hold values from -0.125 to 0.125
Outputs:
- layer_out: bfloat16 [16384, 1024], P(('fsdp', 'tp'))
- input_grad: bfloat16 [16384, 1024], P(('fsdp', 'tp'))
- norm_gain_grad: float32 [1024], replicated
- w_z_grad: float32 [1024, 1536], P('fsdp', 'tp')
- w_x_grad: float32 [1024, 1536], P('fsdp', 'tp')
- w_bc_grad: float32 [1024, 256], P('fsdp')
- w_dt_grad: float32 [1024, 24], P('fsdp', 'tp')
- conv_x_grad: float32 [4, 1536], replicated
- conv_bc_grad: float32 [4, 256], replicated
- dt_bias_grad: float32 [24], replicated
- a_log_grad: float32 [24], replicated
- d_skip_grad: float32 [24], replicated
- w_q_grad: float32 [1024, 512], P('fsdp', 'tp')
- w_k_grad: float32 [1024, 128], P('fsdp', 'tp')
- w_v_grad: float32 [1024, 128], P('fsdp', 'tp')
- w_o_grad: float32 [512, 1024], P('tp', 'fsdp')
- w_out_grad: float32 [1536, 1024], P('tp', 'fsdp')
- ff_gain_grad: float32 [1024], replicated
- w_gate_grad: float32 [1024, 2048], P('fsdp', 'tp')
- w_up_grad: float32 [1024, 2048], P('fsdp', 'tp')
- w_down_grad: float32 [2048, 1024], P('tp', 'fsdp')
Inputs may be any that keep to these rules, and one draw needn't show every extreme that they name: `seq_lengths`: row f holds the 4 document lengths of data shard f in order; they sum to 1024, and the longest of each row is exactly 768.
All inputs are finite; a program needn't handle non-finite values.
Results may differ from a plain program's by a relative error of at most 0.015.
Values may be sent and summed in bfloat16 or wider, within the bound.
A program may use at most 192 MiB of HBM per device.

v0:
```python
from functools import partial
import math

import jax
import jax.numpy as jnp
from jax import lax
from jax.sharding import PartitionSpec as P

HEAD_WIDTH = 64
NS = 128
SPAN = 256
ATT_BLOCK = 512


EPSILON = 1e-05
ROPE_BASE = 10000.0
HIGH = lax.Precision.HIGHEST
MASKED = -1e30


def product(left, right):
    return jnp.dot(left, right, preferred_element_type=jnp.float32)


def product_t(left, right):
    return lax.dot_general(
        left, right, (((1,), (1,)), ((), ())), preferred_element_type=jnp.float32
    )


def product_tn(left, right):
    return lax.dot_general(
        left, right, (((0,), (0,)), ((), ())), preferred_element_type=jnp.float32
    )


def doc_tables(lengths, row_count):
    ends = jnp.cumsum(lengths)
    index = jnp.arange(row_count, dtype=jnp.int32)
    segment = jnp.sum((index[:, None] >= ends[None, :]).astype(jnp.int32), axis=1)
    starts = ends - lengths
    member = segment[:, None] == jnp.arange(lengths.shape[0], dtype=jnp.int32)[None, :]
    begin = jnp.sum(jnp.where(member, starts[None, :], 0), axis=1)
    return (segment, index - begin)


def rms_scale(values, gain):
    factor = lax.rsqrt(jnp.mean(values * values, axis=-1, keepdims=True) + EPSILON)
    return values * factor * gain


def swiglu(gate, upward):
    return jax.nn.silu(gate) * upward


def causal_conv(values, taps, segment):
    width = taps.shape[0]
    total = values * taps[width - 1]
    for delay in range(1, width):
        earlier = jnp.concatenate(
            [jnp.zeros((delay, values.shape[1]), values.dtype), values[:-delay]], axis=0
        )
        joined = jnp.concatenate(
            [
                jnp.zeros((delay,), values.dtype),
                (segment[delay:] == segment[:-delay]).astype(values.dtype),
            ]
        )
        total = total + earlier * joined[:, None] * taps[width - 1 - delay]
    return total


def rotate(values, position):
    row_count = values.shape[0]
    shaped = values.reshape(row_count, -1, HEAD_WIDTH)
    halfway = HEAD_WIDTH // 2
    frequency = ROPE_BASE ** (-2.0 * jnp.arange(halfway, dtype=jnp.float32) / HEAD_WIDTH)
    angle = position.astype(jnp.float32)[:, None, None] * frequency[None, None, :]
    cosine = jnp.cos(angle)
    sine = jnp.sin(angle)
    first = shaped[..., :halfway]
    second = shaped[..., halfway:]
    turned = jnp.concatenate(
        [first * cosine - second * sine, second * cosine + first * sine], axis=-1
    )
    return turned.reshape(row_count, -1)


def span_scan(x_heads, b_vectors, c_vectors, step_size, rate, segment):
    row_count, heads, head_size = x_heads.shape
    count = row_count // SPAN
    inside = jnp.arange(SPAN, dtype=jnp.int32)
    lower = inside[:, None] >= inside[None, :]

    def advance(carry, item):
        state, previous = carry
        block_x, block_b, block_c, block_step, block_seg = item
        decay_factor = jnp.cumsum(block_step * rate[None, :], axis=0)
        allowed = lower & (block_seg[:, None] == block_seg[None, :])
        spread = jnp.where(
            allowed[:, :, None], decay_factor[:, None, :] - decay_factor[None, :, :], MASKED
        )
        inner = jnp.dot(block_c, block_b.T, precision=HIGH, preferred_element_type=jnp.float32)
        mixing = jnp.exp(spread) * inner[:, :, None] * block_step[None, :, :]
        output = jnp.einsum("tsh,shp->thp", mixing, block_x, precision=HIGH)
        carried = (block_seg == previous).astype(jnp.float32)[:, None] * jnp.exp(decay_factor)
        output = (
            output + jnp.einsum("tn,hpn->thp", block_c, state, precision=HIGH) * carried[:, :, None]
        )
        tail = (
            (block_seg == block_seg[-1]).astype(jnp.float32)[:, None]
            * jnp.exp(decay_factor[-1][None, :] - decay_factor)
            * block_step
        )
        state = state * carried[-1][:, None, None] + jnp.einsum(
            "sh,shp,sn->hpn", tail, block_x, block_b, precision=HIGH
        )
        return ((state, block_seg[-1]), output)

    items = (
        x_heads.reshape(count, SPAN, heads, head_size),
        b_vectors.reshape(count, SPAN, -1),
        c_vectors.reshape(count, SPAN, -1),
        step_size.reshape(count, SPAN, heads),
        segment.reshape(count, SPAN),
    )
    start = (
        jnp.zeros((heads, head_size, b_vectors.shape[1]), jnp.float32),
        jnp.asarray(-1, jnp.int32),
    )
    _, outputs = lax.scan(jax.checkpoint(advance), start, items)
    return outputs.reshape(row_count, heads, head_size)


def mixer_middle(
    z_branch, x_branch, pair_branch, step_raw, conv_own, conv_pair, bias, log_rate, skip, segment
):
    row_count = z_branch.shape[0]
    x_active = jax.nn.silu(causal_conv(x_branch, conv_own, segment))
    pair_active = jax.nn.silu(causal_conv(pair_branch, conv_pair, segment))
    step_size = jax.nn.softplus(step_raw + bias[None, :])
    rate = -jnp.exp(log_rate)
    heads = bias.shape[0]
    x_heads = x_active.reshape(row_count, heads, HEAD_WIDTH)
    states = span_scan(x_heads, pair_active[:, :NS], pair_active[:, NS:], step_size, rate, segment)
    result = states + skip[None, :, None] * x_heads
    return result.reshape(row_count, heads * HEAD_WIDTH) * jax.nn.silu(z_branch)


def attend_forward(query, keys, values, segment):
    row_count = query.shape[0]
    kv_heads = keys.shape[1] // HEAD_WIDTH
    group = query.shape[1] // keys.shape[1]
    key_heads = keys.reshape(row_count, kv_heads, HEAD_WIDTH)
    value_heads = values.reshape(row_count, kv_heads, HEAD_WIDTH)
    index = jnp.arange(row_count, dtype=jnp.int32)
    count = row_count // ATT_BLOCK
    scale = 1.0 / math.sqrt(HEAD_WIDTH)

    def block(item):
        query_block, seg_block, row_block = item
        score = (
            jnp.einsum("qkgd,skd->kgqs", query_block, key_heads, preferred_element_type=jnp.float32)
            * scale
        )
        allowed = (seg_block[:, None] == segment[None, :]) & (row_block[:, None] >= index[None, :])
        score = jnp.where(allowed[None, None], score, MASKED)
        peak = jnp.max(score, axis=-1, keepdims=True)
        weight = jnp.exp(score - peak)
        total = jnp.sum(weight, axis=-1, keepdims=True)
        prob = (weight / total).astype(jnp.bfloat16)
        output = jnp.einsum("kgqs,skd->qkgd", prob, value_heads, preferred_element_type=jnp.float32)
        return (
            output.reshape(ATT_BLOCK, kv_heads * group * HEAD_WIDTH),
            (peak + jnp.log(total))[..., 0],
        )

    blocks = (
        query.reshape(count, ATT_BLOCK, kv_heads, group, HEAD_WIDTH),
        segment.reshape(count, ATT_BLOCK),
        index.reshape(count, ATT_BLOCK),
    )
    outputs, logsum = lax.map(block, blocks)
    return (outputs.reshape(row_count, -1), logsum)


def attend_backward(query, keys, values, segment, logsum, attended_grad):
    row_count = query.shape[0]
    kv_heads = keys.shape[1] // HEAD_WIDTH
    group = query.shape[1] // keys.shape[1]
    key_heads = keys.reshape(row_count, kv_heads, HEAD_WIDTH)
    value_heads = values.reshape(row_count, kv_heads, HEAD_WIDTH)
    index = jnp.arange(row_count, dtype=jnp.int32)
    count = row_count // ATT_BLOCK
    scale = 1.0 / math.sqrt(HEAD_WIDTH)

    def block(carry, item):
        key_total, value_total = carry
        query_block, seg_block, row_block, logsum_block, grad_block = item
        score = (
            jnp.einsum("qkgd,skd->kgqs", query_block, key_heads, preferred_element_type=jnp.float32)
            * scale
        )
        allowed = (seg_block[:, None] == segment[None, :]) & (row_block[:, None] >= index[None, :])
        score = jnp.where(allowed[None, None], score, MASKED)
        prob = jnp.exp(score - logsum_block[..., None])
        prob_low = prob.astype(jnp.bfloat16)
        prob_grad = jnp.einsum(
            "qkgd,skd->kgqs", grad_block, value_heads, preferred_element_type=jnp.float32
        )
        centre = jnp.sum(prob * prob_grad, axis=-1, keepdims=True)
        score_grad = (prob * (prob_grad - centre)).astype(jnp.bfloat16)
        query_grad = (
            jnp.einsum("kgqs,skd->qkgd", score_grad, key_heads, preferred_element_type=jnp.float32)
            * scale
        )
        key_total = (
            key_total
            + jnp.einsum(
                "kgqs,qkgd->skd", score_grad, query_block, preferred_element_type=jnp.float32
            )
            * scale
        )
        value_total = value_total + jnp.einsum(
            "kgqs,qkgd->skd", prob_low, grad_block, preferred_element_type=jnp.float32
        )
        return ((key_total, value_total), query_grad.reshape(ATT_BLOCK, -1))

    blocks = (
        query.reshape(count, ATT_BLOCK, kv_heads, group, HEAD_WIDTH),
        segment.reshape(count, ATT_BLOCK),
        index.reshape(count, ATT_BLOCK),
        logsum,
        attended_grad.reshape(count, ATT_BLOCK, kv_heads, group, HEAD_WIDTH),
    )
    empty = jnp.zeros((row_count, kv_heads, HEAD_WIDTH), jnp.float32)
    (key_total, value_total), query_grads = lax.scan(block, (empty, empty), blocks)
    return (
        query_grads.reshape(row_count, -1),
        key_total.reshape(row_count, -1),
        value_total.reshape(row_count, -1),
    )


def shards(
    hidden_in,
    out_grad,
    seq_lengths,
    norm_gain,
    w_z,
    w_x,
    w_bc,
    w_dt,
    conv_x,
    conv_bc,
    dt_bias,
    a_log,
    d_skip,
    w_q,
    key_matrix,
    value_matrix,
    w_o,
    w_out,
    ff_gain,
    w_gate,
    w_up,
    w_down,
):
    pieces = lax.axis_size("tp")
    place = lax.axis_index("tp")
    resident = hidden_in.astype(jnp.float32)
    own_rows = resident.shape[0]
    row_count = own_rows * pieces
    segment, position = doc_tables(seq_lengths[0], row_count)
    width_here = w_x.shape[1]
    heads_here = w_dt.shape[1]
    conv_here = lax.dynamic_slice_in_dim(conv_x, place * width_here, width_here, 1)
    bias_here = lax.dynamic_slice_in_dim(dt_bias, place * heads_here, heads_here, 0)
    rate_here = lax.dynamic_slice_in_dim(a_log, place * heads_here, heads_here, 0)
    skip_here = lax.dynamic_slice_in_dim(d_skip, place * heads_here, heads_here, 0)
    full_z, full_x, full_bc, full_dt, full_q, full_k, full_v, full_o, full_out = (
        lax.all_gather(w_z, "fsdp", axis=0, tiled=True),
        lax.all_gather(w_x, "fsdp", axis=0, tiled=True),
        lax.all_gather(w_bc, "fsdp", axis=0, tiled=True),
        lax.all_gather(w_dt, "fsdp", axis=0, tiled=True),
        lax.all_gather(w_q, "fsdp", axis=0, tiled=True),
        lax.all_gather(key_matrix, "fsdp", axis=0, tiled=True),
        lax.all_gather(value_matrix, "fsdp", axis=0, tiled=True),
        lax.all_gather(w_o, "fsdp", axis=1, tiled=True),
        lax.all_gather(w_out, "fsdp", axis=1, tiled=True),
    )
    normed_own, norm_pull = jax.vjp(rms_scale, resident, norm_gain)
    normed = lax.all_gather(normed_own.astype(jnp.bfloat16), "tp", axis=0, tiled=True)
    z_branch = product(normed, full_z)
    x_branch = product(normed, full_x)
    pair_branch = product(normed, full_bc)
    step_raw = product(normed, full_dt)
    gated, mixer_pull = jax.vjp(
        partial(mixer_middle, segment=segment),
        z_branch,
        x_branch,
        pair_branch,
        step_raw,
        conv_here,
        conv_bc,
        bias_here,
        rate_here,
        skip_here,
    )
    gated_low = gated.astype(jnp.bfloat16)
    query_rot, query_pull = jax.vjp(partial(rotate, position=position), product(normed, full_q))
    key_rot, key_pull = jax.vjp(partial(rotate, position=position), product(normed, full_k))
    query = query_rot.astype(jnp.bfloat16)
    keys = key_rot.astype(jnp.bfloat16)
    values = product(normed, full_v).astype(jnp.bfloat16)
    attended, logsum = attend_forward(query, keys, values, segment)
    attended_low = attended.astype(jnp.bfloat16)
    branch_terms = product(gated_low, full_out) + product(attended_low, full_o)
    branch_own = lax.psum_scatter(branch_terms, "tp", scatter_dimension=0, tiled=True)
    middle = resident + branch_own
    normed2_own, norm2_pull = jax.vjp(rms_scale, middle, ff_gain)
    normed2 = lax.all_gather(normed2_own.astype(jnp.bfloat16), "tp", axis=0, tiled=True)
    full_gate, full_up, full_down = (
        lax.all_gather(w_gate, "fsdp", axis=0, tiled=True),
        lax.all_gather(w_up, "fsdp", axis=0, tiled=True),
        lax.all_gather(w_down, "fsdp", axis=1, tiled=True),
    )
    gate = product(normed2, full_gate)
    upward = product(normed2, full_up)
    activated, swiglu_pull = jax.vjp(swiglu, gate, upward)
    activated_low = activated.astype(jnp.bfloat16)
    feedforward_local = lax.psum_scatter(
        product(activated_low, full_down).astype(jnp.bfloat16),
        "tp",
        scatter_dimension=0,
        tiled=True,
    ).astype(jnp.float32)
    layer_out = (middle + feedforward_local).astype(jnp.bfloat16)
    cotangent_full = lax.all_gather(out_grad, "tp", axis=0, tiled=True)
    gate_grad, up_grad = swiglu_pull(product_t(cotangent_full, full_down))
    gate_low = gate_grad.astype(jnp.bfloat16)
    up_low = up_grad.astype(jnp.bfloat16)
    normed2_terms = product_t(gate_low, full_gate) + product_t(up_low, full_up)
    gate_term = product_tn(normed2, gate_low)
    up_term = product_tn(normed2, up_low)
    down_term = product_tn(activated_low, cotangent_full)
    gate_wgrad, up_wgrad, down_wgrad = (
        lax.psum_scatter(gate_term, "fsdp", scatter_dimension=0, tiled=True),
        lax.psum_scatter(up_term, "fsdp", scatter_dimension=0, tiled=True),
        lax.psum_scatter(down_term, "fsdp", scatter_dimension=1, tiled=True),
    )
    normed2_grad = lax.psum_scatter(
        normed2_terms.astype(jnp.bfloat16), "tp", scatter_dimension=0, tiled=True
    ).astype(jnp.float32)
    middle_from_norm, ff_gain_grad = norm2_pull(normed2_grad)
    middle_grad = out_grad.astype(jnp.float32) + middle_from_norm
    branch_full = lax.all_gather(middle_grad.astype(jnp.bfloat16), "tp", axis=0, tiled=True)
    out_term = product_tn(gated_low, branch_full)
    o_term = product_tn(attended_low, branch_full)
    attended_grad = product_t(branch_full, full_o).astype(jnp.bfloat16)
    gated_grad = product_t(branch_full, full_out)
    (
        z_grad,
        x_grad,
        pair_grad,
        step_grad,
        conv_grad,
        conv_pair_grad,
        bias_grad,
        rate_grad,
        skip_grad,
    ) = mixer_pull(gated_grad)
    query_grad_rot, key_grad_rot, value_grad = attend_backward(
        query, keys, values, segment, logsum, attended_grad
    )
    (query_grad,) = query_pull(query_grad_rot)
    (key_grad,) = key_pull(key_grad_rot)
    z_low = z_grad.astype(jnp.bfloat16)
    x_low = x_grad.astype(jnp.bfloat16)
    step_low = step_grad.astype(jnp.bfloat16)
    query_low = query_grad.astype(jnp.bfloat16)
    key_low = key_grad.astype(jnp.bfloat16)
    value_low = value_grad.astype(jnp.bfloat16)
    normed_terms = (
        product_t(z_low, full_z)
        + product_t(x_low, full_x)
        + product_t(step_low, full_dt)
        + product_t(query_low, full_q)
        + product_t(key_low, full_k)
        + product_t(value_low, full_v)
        + jnp.dot(
            pair_grad,
            full_bc.astype(jnp.float32).T,
            precision=HIGH,
            preferred_element_type=jnp.float32,
        )
    )
    normed_grad = lax.psum_scatter(
        normed_terms.astype(jnp.bfloat16), "tp", scatter_dimension=0, tiled=True
    ).astype(jnp.float32)
    resident_from_norm, gain_grad = norm_pull(normed_grad)
    input_grad = (middle_grad + resident_from_norm).astype(jnp.bfloat16)
    z_term = product_tn(normed, z_low)
    x_term = product_tn(normed, x_low)
    step_term = product_tn(normed, step_low)
    query_term = product_tn(normed, query_low)
    key_term = product_tn(normed, key_low)
    value_term = product_tn(normed, value_low)
    pair_wgrad = jnp.matmul(normed.T, pair_grad, precision=HIGH)
    (
        z_wgrad,
        x_wgrad,
        step_wgrad,
        query_wgrad,
        key_wgrad,
        value_weight_gradient,
        o_wgrad,
        out_wgrad,
    ) = (
        lax.psum_scatter(z_term, "fsdp", scatter_dimension=0, tiled=True),
        lax.psum_scatter(x_term, "fsdp", scatter_dimension=0, tiled=True),
        lax.psum_scatter(step_term, "fsdp", scatter_dimension=0, tiled=True),
        lax.psum_scatter(query_term, "fsdp", scatter_dimension=0, tiled=True),
        lax.psum_scatter(key_term, "fsdp", scatter_dimension=0, tiled=True),
        lax.psum_scatter(value_term, "fsdp", scatter_dimension=0, tiled=True),
        lax.psum_scatter(o_term, "fsdp", scatter_dimension=1, tiled=True),
        lax.psum_scatter(out_term, "fsdp", scatter_dimension=1, tiled=True),
    )
    conv_full = lax.dynamic_update_slice_in_dim(
        jnp.zeros(conv_x.shape, jnp.float32), conv_grad, place * width_here, 1
    )
    bias_full = lax.dynamic_update_slice_in_dim(
        jnp.zeros(dt_bias.shape, jnp.float32), bias_grad, place * heads_here, 0
    )
    rate_full = lax.dynamic_update_slice_in_dim(
        jnp.zeros(a_log.shape, jnp.float32), rate_grad, place * heads_here, 0
    )
    skip_full = lax.dynamic_update_slice_in_dim(
        jnp.zeros(d_skip.shape, jnp.float32), skip_grad, place * heads_here, 0
    )
    (
        gain_total,
        pair_total,
        conv_total,
        conv_pair_total,
        bias_total,
        rate_total,
        skip_total,
        ff_gain_total,
    ) = lax.psum(
        (
            gain_grad,
            pair_wgrad,
            conv_full,
            conv_pair_grad,
            bias_full,
            rate_full,
            skip_full,
            ff_gain_grad,
        ),
        ("fsdp", "tp"),
    )
    shard_rows = w_bc.shape[0]
    pair_shard = lax.dynamic_slice_in_dim(
        pair_total, lax.axis_index("fsdp") * shard_rows, shard_rows, 0
    )
    return (
        layer_out,
        input_grad,
        gain_total,
        z_wgrad,
        x_wgrad,
        pair_shard,
        step_wgrad,
        conv_total,
        conv_pair_total,
        bias_total,
        rate_total,
        skip_total,
        query_wgrad,
        key_wgrad,
        value_weight_gradient,
        o_wgrad,
        out_wgrad,
        ff_gain_total,
        gate_wgrad,
        up_wgrad,
        down_wgrad,
    )


def solution(mesh):
    in_specs = (
        P(("fsdp", "tp"), None),
        P(("fsdp", "tp"), None),
        P("fsdp", None),
        P(),
        P("fsdp", "tp"),
        P("fsdp", "tp"),
        P("fsdp", None),
        P("fsdp", "tp"),
        P(),
        P(),
        P(),
        P(),
        P(),
        P("fsdp", "tp"),
        P("fsdp", "tp"),
        P("fsdp", "tp"),
        P("tp", "fsdp"),
        P("tp", "fsdp"),
        P(),
        P("fsdp", "tp"),
        P("fsdp", "tp"),
        P("tp", "fsdp"),
    )
    out_specs = (
        P(("fsdp", "tp"), None),
        P(("fsdp", "tp"), None),
        P(),
        P("fsdp", "tp"),
        P("fsdp", "tp"),
        P("fsdp", None),
        P("fsdp", "tp"),
        P(),
        P(),
        P(),
        P(),
        P(),
        P("fsdp", "tp"),
        P("fsdp", "tp"),
        P("fsdp", "tp"),
        P("tp", "fsdp"),
        P("tp", "fsdp"),
        P(),
        P("fsdp", "tp"),
        P("fsdp", "tp"),
        P("tp", "fsdp"),
    )
    return jax.shard_map(shards, mesh=mesh, in_specs=in_specs, out_specs=out_specs, check_vma=False)
```

profile of v0, /device:TPU:0, one launch (start us, length us, event | category | flops | bytes accessed | tf_op | source)
XLA Modules:
  0.0 2447.1 jit_solution(17994924916264459434)
XLA Ops:
  18.7 42.7 %all-gather = bf16[16,64,12]{1,2,0:T(8,128)(2,1)S(1)} all-gather(bf16[1,64,12]{1,2,0:T(8,128)(2,1)S(1)} %bitcast.700), channel_id=1, replica_groups=mesh['fsdp'=16,'tp'=2] {'fsdp'}, dimensions={0}, use_global_device_ids=true | all-gather | bytes 26112 | tf_op jit(solution)/shard_map/all_gather | solution.py:285
  62.2 37.6 %all_gather.55 = bf16[1024,64]{1,0:T(8,128)(2,1)S(1)} all-gather(bf16[64,64]{1,0:T(8,128)(2,1)S(1)} %copy-done.114), channel_id=1, replica_groups=mesh['fsdp'=16,'tp'=2] {'fsdp'}, dimensions={0}, use_global_device_ids=true | all-gather | bytes 139264 | tf_op jit(solution)/shard_map/all_gather | solution.py:287
  99.8 41.5 %all_gather.56 = bf16[1024,64]{1,0:T(8,128)(2,1)} all-gather(bf16[64,64]{1,0:T(8,128)(2,1)S(1)} %copy-done.115), channel_id=1, replica_groups=mesh['fsdp'=16,'tp'=2] {'fsdp'}, dimensions={0}, use_global_device_ids=true | all-gather | bytes 139264 | tf_op jit(solution)/shard_map/all_gather | solution.py:288
  141.3 41.6 %all_gather.51 = bf16[1024,256]{1,0:T(8,128)(2,1)} all-gather(bf16[64,256]{1,0:T(8,128)(2,1)S(1)} %copy-done.97), channel_id=1, replica_groups=mesh['fsdp'=16,'tp'=2] {'fsdp'}, dimensions={0}, use_global_device_ids=true | all-gather | bytes 557056 | tf_op jit(solution)/shard_map/all_gather | solution.py:284
  183.0 42.7 %all_gather.54 = bf16[1024,256]{1,0:T(8,128)(2,1)S(1)} all-gather(bf16[64,256]{1,0:T(8,128)(2,1)S(1)} %copy-done.98), channel_id=1, replica_groups=mesh['fsdp'=16,'tp'=2] {'fsdp'}, dimensions={0}, use_global_device_ids=true | all-gather | bytes 557056 | tf_op jit(solution)/shard_map/all_gather | solution.py:286
  225.7 40.7 %all_gather.57 = bf16[256,1024]{0,1:T(8,128)(2,1)} all-gather(bf16[256,64]{0,1:T(8,128)(2,1)S(1)} %copy-done.99), channel_id=1, replica_groups=mesh['fsdp'=16,'tp'=2] {'fsdp'}, dimensions={1}, use_global_device_ids=true | all-gather | bytes 557056 | tf_op jit(solution)/shard_map/all_gather | solution.py:289
  283.5 21.9 while.73
  333.8 146.2 %while.74 = (s32[]{:T(128)}, f32[12,64,128]{2,1,0:T(8,128)S(1)}, s32[]{:T(128)}, f32[4,256,12,64]{1,0,3,2:T(4,128)}, f32[4,12,64,128]{3,2,1,0:T(8,128)}, /*index...) while((s32[]{:T(128)}, f32[12,64,128]{2,1,0:T(8,128)S(1)}, ...), condition=%wide.region_6.7_spmd.clone, body=%wide.region_3.6_spmd.clone.sunk | while | flops 1313456128 | bytes 10579744 | solution.py:131
  352.2 17.9 dynamic_update_slice.113
  388.6 17.9 dynamic_update_slice.113
  425.0 17.9 dynamic_update_slice.113
  461.5 17.9 dynamic_update_slice.113
  501.7 9.2 reduce-scatter.18.cloned.1.call-done
  516.6 59.3 %all-gather.24.cloned.1.call-done = bf16[1024,1024]{1,0:T(8,128)(2,1)} async-done(((bf16[64,1024]{1,0:T(8,128)(2,1)}), bf16[1024,1024]{1,0:T(8,128)(2,1)}) %all-gather.24.cloned.1.call-update) | async-done | bytes 2097168 | tf_op jit(solution)/shard_map/all_gather | solution.py:325
  575.9 11.5 all-gather.20.cloned.1.call-done
  587.4 6.6 fusion.238
  593.9 58.5 %all-gather.22.cloned.1.call-done = bf16[1024,1024]{1,0:T(8,128)(2,1)} async-done(((bf16[64,1024]{1,0:T(8,128)(2,1)}), bf16[1024,1024]{1,0:T(8,128)(2,1)}) %all-gather.22.cloned.1.call-update) | async-done | bytes 2097168 | tf_op jit(solution)/shard_map/all_gather | solution.py:324
  663.3 64.9 %all-gather.26.cloned.1.call-done = bf16[1024,1024]{0,1:T(8,128)(2,1)} async-done(((bf16[1024,64]{0,1:T(8,128)(2,1)}), bf16[1024,1024]{0,1:T(8,128)(2,1)}) %all-gather.26.cloned.1.call-update) | async-done | bytes 2097168 | tf_op jit(solution)/shard_map/all_gather | solution.py:326
  728.2 9.9 multiply_convert_fusion
  745.1 8.3 reduce-scatter.22.cloned.1.call-done
  760.4 9.3 all-gather.30.cloned.1.call-done
  769.6 10.2 multiply_reduce_fusion.3
  792.3 317.0 %while.75 = (s32[]{:T(128)}, f32[12]{0:T(128)}, f32[12,64,128]{2,1,0:T(8,128)}, f32[4,256,12,64]{1,0,3,2:T(4,128)}, f32[4,256,128]{2,1,0:T(8,128)}, /*index=5*/f...) while((s32[]{:T(128)}, f32[12]{0:T(128)}, ...), condition=%wide.region_30.31_spmd.clone, body=%wide.region_17.30_spmd.clone.sunk | while | flops 3036590080 | bytes 27178100 | solution.py:131
  852.7 17.9 dynamic_update_slice.117
  932.2 17.9 dynamic_update_slice.117
  1011.7 17.9 dynamic_update_slice.117
  1091.3 17.9 dynamic_update_slice.117
  1121.7 6.9 multiply_reduce_fusion.7
  1140.6 48.2 %while.76 = (s32[]{:T(128)}, f32[1024,1,64]{0,2,1:T(8,128)S(1)}, f32[1024,1,64]{0,2,1:T(8,128)}, f32[2,512,256]{1,0,2:T(2,128)}, bf16[2,512,1,4,64]{1,4,3,2,0:T(...) while((s32[]{:T(128)}, f32[1024,1,64]{0,2,1:T(8,128)S(1)}, ...), condition=%wide.region_33.34_spmd.clone, body=%wide.region_31.33_spmd.clone.sunk | while | flops 1375664128 | bytes 70197416 | solution.py:237
  1153.8 10.3 dynamic_update_slice.119
  1178.3 10.3 dynamic_update_slice.119
  1225.4 8.4 add_convert_fusion
  1249.9 6.6 fusion.251
  1256.6 6.6 fusion.249
  1263.3 6.7 fusion.250
  1288.8 121.5 %all-reduce.33.cloned.1.call-done = f32[1024,256]{1,0:T(8,128)} async-done(((f32[1024,256]{1,0:T(8,128)}), f32[1024,256]{1,0:T(8,128)}) %all-reduce.33.cloned.1.call-update) | async-done | bytes 1048592 | tf_op jit(solution)/shard_map/psum | solution.py:450
  1411.8 9.2 reduce-scatter.24.cloned.1.call-done
  1423.2 41.8 %all-reduce.30 = (f32[1024]{0:T(1024)}, f32[4,1536]{1,0:T(4,128)}, f32[4,256]{1,0:T(4,128)}, f32[24]{0:T(128)}, f32[24]{0:T(128)}, /*index=5*/f32[24]{0:T(128)}, f32[1024]{0:T(1024)}) all-reduce(f32[1024]{0:T(1024)S(1)} %get-tuple-element.1027, ...), channel_id=1, replica_groups=mesh['fsdp'=16,'tp'=2] {'fsdp','tp'}, use_global_device_ids=true, to_apply=%region_37.38 | all-reduce | flops 9288 | bytes 74304 | tf_op jit(solution)/shard_map/psum | solution.py:450
  1469.1 45.4 %reduce-scatter.32.cloned.1.call-done = f32[64,64]{1,0:T(8,128)} async-done(((f32[1024,64]{1,0:T(8,128)}), f32[64,64]{1,0:T(8,128)}) %reduce-scatter.32.cloned.1.call-update) | async-done | bytes 16400 | tf_op jit(solution)/shard_map/reduce_scatter | solution.py:424
  1514.5 75.7 %reduce-scatter.34.cloned.1.call-done = f32[64,64]{1,0:T(8,128)} async-done(((f32[1024,64]{1,0:T(8,128)}), f32[64,64]{1,0:T(8,128)}) %reduce-scatter.34.cloned.1.call-update) | async-done | bytes 16400 | tf_op jit(solution)/shard_map/reduce_scatter | solution.py:425
  1590.2 76.9 %reduce-scatter.36.cloned.1.call-done = f32[256,64]{0,1:T(8,128)} async-done(((f32[256,1024]{0,1:T(8,128)}), f32[256,64]{0,1:T(8,128)}) %reduce-scatter.36.cloned.1.call-update) | async-done | bytes 65552 | tf_op jit(solution)/shard_map/reduce_scatter | solution.py:426
  1667.1 77.0 %reduce-scatter.30.cloned.1.call-done = f32[64,256]{1,0:T(8,128)} async-done(((f32[1024,256]{1,0:T(8,128)}), f32[64,256]{1,0:T(8,128)}) %reduce-scatter.30.cloned.1.call-update) | async-done | bytes 65552 | tf_op jit(solution)/shard_map/reduce_scatter | solution.py:423
  1744.1 94.6 %reduce-scatter.44.cloned.1.call-done = f32[1024,64]{0,1:T(8,128)} async-done(((f32[1024,1024]{0,1:T(8,128)}), f32[1024,64]{0,1:T(8,128)}) %reduce-scatter.44.cloned.1.call-update) | async-done | bytes 262160 | tf_op jit(solution)/shard_map/reduce_scatter | solution.py:350
  1838.7 97.6 %reduce-scatter.40.cloned.1.call-done = f32[64,1024]{1,0:T(8,128)} async-done(((f32[1024,1024]{1,0:T(8,128)}), f32[64,1024]{1,0:T(8,128)}) %reduce-scatter.40.cloned.1.call-update) | async-done | bytes 262160 | tf_op jit(solution)/shard_map/reduce_scatter | solution.py:348
  1936.3 97.6 %reduce-scatter.42.cloned.1.call-done = f32[64,1024]{1,0:T(8,128)} async-done(((f32[1024,1024]{1,0:T(8,128)}), f32[64,1024]{1,0:T(8,128)}) %reduce-scatter.42.cloned.1.call-update) | async-done | bytes 262160 | tf_op jit(solution)/shard_map/reduce_scatter | solution.py:349
  2033.9 135.4 %reduce-scatter.38.cloned.1.call-done = f32[768,64]{0,1:T(8,128)} async-done(((f32[768,1024]{0,1:T(8,128)}), f32[768,64]{0,1:T(8,128)}) %reduce-scatter.38.cloned.1.call-update) | async-done | bytes 196624 | tf_op jit(solution)/shard_map/reduce_scatter | solution.py:427
  2169.4 135.4 %reduce-scatter.26.cloned.1.call-done = f32[64,768]{1,0:T(8,128)} async-done(((f32[1024,768]{1,0:T(8,128)}), f32[64,768]{1,0:T(8,128)}) %reduce-scatter.26.cloned.1.call-update) | async-done | bytes 196624 | tf_op jit(solution)/shard_map/reduce_scatter | solution.py:420
  2304.8 135.5 %reduce-scatter.28.cloned.1.call-done = f32[64,768]{1,0:T(8,128)} async-done(((f32[1024,768]{1,0:T(8,128)}), f32[64,768]{1,0:T(8,128)}) %reduce-scatter.28.cloned.1.call-update) | async-done | bytes 196624 | tf_op jit(solution)/shard_map/reduce_scatter | solution.py:421
  (896 shorter events, 588.5 us)
Async XLA Ops:
  7.3 54.9 %copy-start.114 = (bf16[64,64]{1,0:T(8,128)(2,1)S(1)}, bf16[64,64]{1,0:T(8,128)(2,1)}, u32[]{:S(2)}) copy-start(bf16[64,64]{1,0:T(8,128)(2,1)} %param.44) | copy-start | bytes 24580
  7.3 92.5 %copy-start.115 = (bf16[64,64]{1,0:T(8,128)(2,1)S(1)}, bf16[64,64]{1,0:T(8,128)(2,1)}, u32[]{:S(2)}) copy-start(bf16[64,64]{1,0:T(8,128)(2,1)} %param.45) | copy-start | bytes 24580
  7.3 134.0 %copy-start.97 = (bf16[64,256]{1,0:T(8,128)(2,1)S(1)}, bf16[64,256]{1,0:T(8,128)(2,1)}, u32[]{:S(2)}) copy-start(bf16[64,256]{1,0:T(8,128)(2,1)} %param.36) | copy-start | bytes 98308
  7.3 175.7 %copy-start.98 = (bf16[64,256]{1,0:T(8,128)(2,1)S(1)}, bf16[64,256]{1,0:T(8,128)(2,1)}, u32[]{:S(2)}) copy-start(bf16[64,256]{1,0:T(8,128)(2,1)} %param.43) | copy-start | bytes 98308
  7.3 261.0 %all-gather.12.cloned.1.call-start = ((), (), s32[]{:S(2)}) async-start(), calls=%async_computation.15 | async-start | bytes 3145728 | tf_op jit(solution)/shard_map/all_gather | solution.py:293
  7.3 218.4 %copy-start.99 = (bf16[256,64]{0,1:T(8,128)(2,1)S(1)}, bf16[256,64]{0,1:T(8,128)(2,1)}, u32[]{:S(2)}) copy-start(bf16[256,64]{0,1:T(8,128)(2,1)} %param.46) | copy-start | bytes 98308
  10.1 257.6 %copy-start.125 = (f32[4,1536]{1,0:T(4,128)S(1)}, f32[4,1536]{1,0:T(4,128)}, u32[]{:S(2)}) copy-start(f32[4,1536]{1,0:T(4,128)} %param.38) | copy-start | bytes 73732
  12.6 298.2 %all-gather.14.cloned.1.call-start = ((), (), s32[]{:S(2)}) async-start(), calls=%async_computation.16 | async-start | bytes 1671168 | tf_op jit(solution)/shard_map/all_gather | solution.py:283
  13.3 474.5 %all-gather.16.cloned.1.call-start = ((), (), s32[]{:S(2)}) async-start(), calls=%async_computation.17 | async-start | bytes 1671168 | tf_op jit(solution)/shard_map/all_gather | solution.py:282
  14.1 480.3 %all-gather.18.cloned.1.call-start = ((), (), s32[]{:S(2)}) async-start(), calls=%async_computation.18 | async-start | bytes 1671168 | tf_op jit(solution)/shard_map/all_gather | solution.py:290
  14.7 496.2 %reduce-scatter.18.cloned.1.call-start = ((), (), s32[]{:S(2)}) async-start(), calls=%async_computation.19 | async-start | bytes 6291456 | tf_op jit(solution)/shard_map/reduce_scatter | solution.py:319
  14.7 253.6 %copy-start.126 = (f32[32]{0:T(128)}, f32[32]{0:T(128)S(1)}, u32[]{:S(2)}) copy-start(f32[32]{0:T(128)S(1)} %multiply_power_fusion) | copy-start | bytes 388
  17.2 740.6 %copy-start.68 = (f32[1024]{0:T(1024)}, f32[1024]{0:T(1024)S(1)}, u32[]{:S(2)}) copy-start(f32[1024]{0:T(1024)S(1)} %pad_convert_fusion.1) | copy-start | bytes 12292
  17.3 251.0 %copy-start.81 = (f32[1024]{0:T(1024)}, f32[1024]{0:T(1024)S(1)}, u32[]{:S(2)}) copy-start(f32[1024]{0:T(1024)S(1)} %subtract_convert_fusion.1) | copy-start | bytes 12292
  99.8 176.8 %copy-start.41 = (bf16[1024,64]{1,0:T(8,128)(2,1)}, bf16[1024,64]{1,0:T(8,128)(2,1)S(1)}, u32[]{:S(2)}) copy-start(bf16[1024,64]{1,0:T(8,128)(2,1)S(1)} %all_gather.55) | copy-start | bytes 393220
  501.0 74.9 %all-gather.24.cloned.1.call-start = ((), (), s32[]{:S(2)}) async-start(), calls=%async_computation.22 | async-start | bytes 2228224 | tf_op jit(solution)/shard_map/all_gather | solution.py:325
  501.6 85.8 %all-gather.20.cloned.1.call-start = ((), (), s32[]{:S(2)}) async-start(), calls=%async_computation.20 | async-start | bytes 3145728 | tf_op jit(solution)/shard_map/all_gather | solution.py:322
  512.8 243.2 %copy-start.8 = (f32[512,1024]{1,0:T(8,128)}, f32[512,1024]{1,0:T(8,128)S(1)}, u32[]{:S(2)}) copy-start(f32[512,1024]{1,0:T(8,128)S(1)} %get-tuple-element.1151) | copy-start | bytes 6291460
  512.8 243.2 %copy-start.83 = (f32[512]{0:T(512)}, f32[512]{0:T(512)S(1)}, u32[]{:S(2)}) copy-start(f32[512]{0:T(512)S(1)} %fusion.219) | copy-start | bytes 6148
  514.3 138.1 %all-gather.22.cloned.1.call-start = ((), (), s32[]{:S(2)}) async-start(), calls=%async_computation.21 | async-start | bytes 2228224 | tf_op jit(solution)/shard_map/all_gather | solution.py:324
  515.1 148.2 %all-gather.28.cloned.1.call-start = ((), (), s32[]{:S(2)}) async-start(), calls=%async_computation.25 | async-start | bytes 3145728 | tf_op jit(solution)/shard_map/all_gather | solution.py:339
  515.8 212.4 %all-gather.26.cloned.1.call-start = ((), (), s32[]{:S(2)}) async-start(), calls=%async_computation.23 | async-start | bytes 2228224 | tf_op jit(solution)/shard_map/all_gather | solution.py:326
  516.4 237.0 %reduce-scatter.22.cloned.1.call-start = ((), (), s32[]{:S(2)}) async-start(), calls=%async_computation.26 | async-start | bytes 3145728 | tf_op jit(solution)/shard_map/reduce_scatter | solution.py:352
  745.0 24.6 %all-gather.30.cloned.1.call-start = ((), (), s32[]{:S(2)}) async-start(), calls=%async_computation.27 | async-start | bytes 3145728 | tf_op jit(solution)/shard_map/all_gather | solution.py:357
  757.7 529.7 %reduce-scatter.46.cloned.1.call-start = ((), (), s32[]{:S(2)}) async-start(), calls=%async_computation.40 | async-start | bytes 557056
  792.3 317.0 %copy-start.7 = (f32[1024,256]{1,0:T(8,128)S(1)}, f32[1024,256]{1,0:T(8,128)}, u32[]{:S(2)}) copy-start(f32[1024,256]{1,0:T(8,128)} %copy-done.6) | copy-start | bytes 3145732
  1199.6 210.7 %all-reduce.33.cloned.1.call-start = ((), (), s32[]{:S(2)}) async-start(), calls=%async_computation.31 | async-start | bytes 2097152 | tf_op jit(solution)/shard_map/psum | solution.py:450
  1209.1 212.0 %reduce-scatter.24.cloned.1.call-start = ((), (), s32[]{:S(2)}) async-start(), calls=%async_computation.28 | async-start | bytes 3145728 | tf_op jit(solution)/shard_map/reduce_scatter | solution.py:398
  1233.8 231.3 %reduce-scatter.20.cloned.1.call-start = ((), (), s32[]{:S(2)}) async-start(), calls=%async_computation.24 | async-start | bytes 3145728 | tf_op jit(solution)/shard_map/reduce_scatter | solution.py:332
  1239.9 274.6 %reduce-scatter.32.cloned.1.call-start = ((), (), s32[]{:S(2)}) async-start(), calls=%async_computation.33 | async-start | bytes 557056 | tf_op jit(solution)/shard_map/reduce_scatter | solution.py:424
  1241.5 348.7 %reduce-scatter.34.cloned.1.call-start = ((), (), s32[]{:S(2)}) async-start(), calls=%async_computation.34 | async-start | bytes 557056 | tf_op jit(solution)/shard_map/reduce_scatter | solution.py:425
  1244.1 423.0 %reduce-scatter.36.cloned.1.call-start = ((), (), s32[]{:S(2)}) async-start(), calls=%async_computation.35 | async-start | bytes 1114112 | tf_op jit(solution)/shard_map/reduce_scatter | solution.py:426
  1247.8 496.3 %reduce-scatter.30.cloned.1.call-start = ((), (), s32[]{:S(2)}) async-start(), calls=%async_computation.32 | async-start | bytes 1114112 | tf_op jit(solution)/shard_map/reduce_scatter | solution.py:423
  1249.8 588.9 %reduce-scatter.44.cloned.1.call-start = ((), (), s32[]{:S(2)}) async-start(), calls=%async_computation.39 | async-start | bytes 4456448 | tf_op jit(solution)/shard_map/reduce_scatter | solution.py:350
  1256.5 679.8 %reduce-scatter.40.cloned.1.call-start = ((), (), s32[]{:S(2)}) async-start(), calls=%async_computation.37 | async-start | bytes 4456448 | tf_op jit(solution)/shard_map/reduce_scatter | solution.py:348
  1263.2 770.7 %reduce-scatter.42.cloned.1.call-start = ((), (), s32[]{:S(2)}) async-start(), calls=%async_computation.38 | async-start | bytes 4456448 | tf_op jit(solution)/shard_map/reduce_scatter | solution.py:349
  1269.9 899.4 %reduce-scatter.38.cloned.1.call-start = ((), (), s32[]{:S(2)}) async-start(), calls=%async_computation.36 | async-start | bytes 3342336 | tf_op jit(solution)/shard_map/reduce_scatter | solution.py:427
  1275.6 1029.2 %reduce-scatter.26.cloned.1.call-start = ((), (), s32[]{:S(2)}) async-start(), calls=%async_computation.29 | async-start | bytes 3342336 | tf_op jit(solution)/shard_map/reduce_scatter | solution.py:420
  1280.6 1159.7 %reduce-scatter.28.cloned.1.call-start = ((), (), s32[]{:S(2)}) async-start(), calls=%async_computation.30 | async-start | bytes 3342336 | tf_op jit(solution)/shard_map/reduce_scatter | solution.py:421
  1285.9 135.2 %copy-start.12 = (bf16[512,1024]{1,0:T(8,128)(2,1)S(1)}, bf16[512,1024]{1,0:T(8,128)(2,1)}, u32[]{:S(2)}) copy-start(bf16[512,1024]{1,0:T(8,128)(2,1)} %param.30) | copy-start | bytes 3145732
  1285.9 135.2 %copy-start.85 = (f32[1024]{0:T(1024)S(1)}, f32[1024]{0:T(1024)}, u32[]{:S(2)}) copy-start(f32[1024]{0:T(1024)} %param.33) | copy-start | bytes 12292
  1285.9 135.2 %copy-start.101 = (f32[512]{0:T(512)S(1)}, f32[512]{0:T(512)}, u32[]{:S(2)}) copy-start(f32[512]{0:T(512)} %copy-done.100) | copy-start | bytes 6148
  1285.9 137.3 %copy-start.107 = (f32[1024]{0:T(1024)S(1)}, f32[1024]{0:T(1024)}, u32[]{:S(2)}) copy-start(f32[1024]{0:T(1024)} %get-tuple-element.1021) | copy-start | bytes 12292
  1285.9 179.1 %copy-start.105 = (f32[512]{0:T(512)S(1)}, f32[512]{0:T(512)}, u32[]{:S(2)}) copy-start(f32[512]{0:T(512)} %copy-done.104) | copy-start | bytes 6148
  1285.9 179.1 %copy-start.9 = (f32[512,1024]{1,0:T(8,128)S(1)}, f32[512,1024]{1,0:T(8,128)}, u32[]{:S(2)}) copy-start(f32[512,1024]{1,0:T(8,128)} %copy-done.8) | copy-start | bytes 6291460
  1285.9 179.1 %copy-start.80 = (f32[1024]{0:T(1024)S(1)}, f32[1024]{0:T(1024)}, u32[]{:S(2)}) copy-start(f32[1024]{0:T(1024)} %param.48) | copy-start | bytes 12292
  1286.0 179.1 %copy-start.84 = (f32[512]{0:T(512)S(1)}, f32[512]{0:T(512)}, u32[]{:S(2)}) copy-start(f32[512]{0:T(512)} %copy-done.83) | copy-start | bytes 6148
  1286.0 179.1 %copy-start.103 = (f32[512]{0:T(512)S(1)}, f32[512]{0:T(512)}, u32[]{:S(2)}) copy-start(f32[512]{0:T(512)} %copy-done.102) | copy-start | bytes 6148
  (149 other events, 753.1 us)
Sparse Core Ops, SparseCore 0:
  12.7 13.2 all-gather.11
  28.8 60.0 all-gather.13
  91.6 59.8 all-gather.15
  154.2 59.5 all-gather.17
  501.1 9.7 reduce-scatter.17
  513.9 61.9 all-gather.23
  578.1 9.2 all-gather.19
  590.5 61.8 all-gather.21
  654.1 9.2 all-gather.27
  666.3 61.8 all-gather.25
  745.2 8.2 reduce-scatter.21
  757.8 11.7 all-gather.29
  1199.8 77.8 reduce-scatter.45
  1284.1 126.2 all-reduce.32
  1412.5 8.5 reduce-scatter.23
  1423.3 10.7 reduce-scatter.19
  1436.7 77.7 reduce-scatter.31
  1517.3 72.9 reduce-scatter.33
  1593.1 74.0 reduce-scatter.35
  1669.9 74.1 reduce-scatter.29
  1747.0 91.7 reduce-scatter.43
  1841.6 94.6 reduce-scatter.39
  1939.2 94.6 reduce-scatter.41
  2039.3 129.9 reduce-scatter.37
  2174.9 129.8 reduce-scatter.25
  2310.2 130.0 reduce-scatter.27
where the time goes:
time: 2460 us; the launch traced here: 2450 us
  waiting for transfers between devices  1330 us (54%)
  local copies, waits for them, and re-layouts  344 us (14%)
  matrix products  312 us (13%)
  blocking collectives  289 us (12%)
  other arithmetic  147 us (6%)
    dynamic_update_slice x28, local copies, waits for them, and re-layouts, span_scan(): _, outputs = lax.scan(jax.checkpoint(advance), start, items)  161 us
    reduce_scatter x1, waiting for transfers between devices, shards(): lax.psum_scatter(x_term, 'fsdp', scatter_dimension=0, tiled=True)  135 us
    reduce_scatter x1, waiting for transfers between devices, shards(): lax.psum_scatter(z_term, 'fsdp', scatter_dimension=0, tiled=True)  135 us
    reduce_scatter x1, waiting for transfers between devices, shards(): lax.psum_scatter(out_term, 'fsdp', scatter_dimension=1, tiled=True)  135 us
    psum x1, waiting for transfers between devices, shards(): lax.psum((gain_grad, pair_wgrad, conv_full, conv_pair_grad, bias_full, ra...  122 us
    reduce_scatter x1, waiting for transfers between devices, shards(): lax.psum_scatter(up_term, 'fsdp', scatter_dimension=0, tiled=True)  97.6 us
    reduce_scatter x1, waiting for transfers between devices, shards(): lax.psum_scatter(gate_term, 'fsdp', scatter_dimension=0, tiled=True)  97.6 us
    reduce_scatter x1, waiting for transfers between devices, shards(): lax.psum_scatter(down_term, 'fsdp', scatter_dimension=1, tiled=True)  94.6 us
  transfers between devices with their start and end apart: 26, of which 20 were waited for; matrix products, arithmetic and copies ran while one was open for 14% of the time, Pallas kernels for 0%

commit v1 on v0

--- a/solution.py
+++ b/solution.py
@@ -14,7 +14,7 @@
 
 EPSILON = 1e-05
 ROPE_BASE = 10000.0
-HIGH = lax.Precision.HIGHEST
+HIGH = lax.Precision.HIGH
 MASKED = -1e30
 
 
@@ -42,6 +42,12 @@
     member = segment[:, None] == jnp.arange(lengths.shape[0], dtype=jnp.int32)[None, :]
     begin = jnp.sum(jnp.where(member, starts[None, :], 0), axis=1)
     return (segment, index - begin)
+
+
+def shard_sum(term):
+    return lax.psum_scatter(
+        term.astype(jnp.bfloat16), "fsdp", scatter_dimension=0, tiled=True
+    ).astype(jnp.float32)
 
 
 def rms_scale(values, gain):
@@ -286,8 +292,8 @@
         lax.all_gather(w_q, "fsdp", axis=0, tiled=True),
         lax.all_gather(key_matrix, "fsdp", axis=0, tiled=True),
         lax.all_gather(value_matrix, "fsdp", axis=0, tiled=True),
-        lax.all_gather(w_o, "fsdp", axis=1, tiled=True),
-        lax.all_gather(w_out, "fsdp", axis=1, tiled=True),
+        lax.all_gather(w_o.T, "fsdp", axis=0, tiled=True).T,
+        lax.all_gather(w_out.T, "fsdp", axis=0, tiled=True).T,
     )
     normed_own, norm_pull = jax.vjp(rms_scale, resident, norm_gain)
     normed = lax.all_gather(normed_own.astype(jnp.bfloat16), "tp", axis=0, tiled=True)
@@ -323,7 +329,7 @@
     full_gate, full_up, full_down = (
         lax.all_gather(w_gate, "fsdp", axis=0, tiled=True),
         lax.all_gather(w_up, "fsdp", axis=0, tiled=True),
-        lax.all_gather(w_down, "fsdp", axis=1, tiled=True),
+        lax.all_gather(w_down.T, "fsdp", axis=0, tiled=True).T,
     )
     gate = product(normed2, full_gate)
     upward = product(normed2, full_up)
@@ -343,11 +349,11 @@
     normed2_terms = product_t(gate_low, full_gate) + product_t(up_low, full_up)
     gate_term = product_tn(normed2, gate_low)
     up_term = product_tn(normed2, up_low)
-    down_term = product_tn(activated_low, cotangent_full)
+    down_term = product_tn(cotangent_full, activated_low)
     gate_wgrad, up_wgrad, down_wgrad = (
-        lax.psum_scatter(gate_term, "fsdp", scatter_dimension=0, tiled=True),
-        lax.psum_scatter(up_term, "fsdp", scatter_dimension=0, tiled=True),
-        lax.psum_scatter(down_term, "fsdp", scatter_dimension=1, tiled=True),
+        shard_sum(gate_term),
+        shard_sum(up_term),
+        shard_sum(down_term).T,
     )
     normed2_grad = lax.psum_scatter(
         normed2_terms.astype(jnp.bfloat16), "tp", scatter_dimension=0, tiled=True
@@ -355,8 +361,8 @@
     middle_from_norm, ff_gain_grad = norm2_pull(normed2_grad)
     middle_grad = out_grad.astype(jnp.float32) + middle_from_norm
     branch_full = lax.all_gather(middle_grad.astype(jnp.bfloat16), "tp", axis=0, tiled=True)
-    out_term = product_tn(gated_low, branch_full)
-    o_term = product_tn(attended_low, branch_full)
+    out_term = product_tn(branch_full, gated_low)
+    o_term = product_tn(branch_full, attended_low)
     attended_grad = product_t(branch_full, full_o).astype(jnp.bfloat16)
     gated_grad = product_t(branch_full, full_out)
     (
@@ -417,14 +423,14 @@
         o_wgrad,
         out_wgrad,
     ) = (
-        lax.psum_scatter(z_term, "fsdp", scatter_dimension=0, tiled=True),
-        lax.psum_scatter(x_term, "fsdp", scatter_dimension=0, tiled=True),
-        lax.psum_scatter(step_term, "fsdp", scatter_dimension=0, tiled=True),
-        lax.psum_scatter(query_term, "fsdp", scatter_dimension=0, tiled=True),
-        lax.psum_scatter(key_term, "fsdp", scatter_dimension=0, tiled=True),
-        lax.psum_scatter(value_term, "fsdp", scatter_dimension=0, tiled=True),
-        lax.psum_scatter(o_term, "fsdp", scatter_dimension=1, tiled=True),
-        lax.psum_scatter(out_term, "fsdp", scatter_dimension=1, tiled=True),
+        shard_sum(z_term),
+        shard_sum(x_term),
+        shard_sum(step_term),
+        shard_sum(query_term),
+        shard_sum(key_term),
+        shard_sum(value_term),
+        shard_sum(o_term).T,
+        shard_sum(out_term).T,
     )
     conv_full = lax.dynamic_update_slice_in_dim(
         jnp.zeros(conv_x.shape, jnp.float32), conv_grad, place * width_here, 1
@@ -440,7 +446,6 @@
     )
     (
         gain_total,
-        pair_total,
         conv_total,
         conv_pair_total,
         bias_total,
@@ -450,7 +455,6 @@
     ) = lax.psum(
         (
             gain_grad,
-            pair_wgrad,
             conv_full,
             conv_pair_grad,
             bias_full,
@@ -460,10 +464,7 @@
         ),
         ("fsdp", "tp"),
     )
-    shard_rows = w_bc.shape[0]
-    pair_shard = lax.dynamic_slice_in_dim(
-        pair_total, lax.axis_index("fsdp") * shard_rows, shard_rows, 0
-    )
+    pair_shard = lax.psum(shard_sum(pair_wgrad), "tp")
     return (
         layer_out,
         input_grad,

time: 2460 us -> 2020 us (0.82)
  waiting for transfers between devices: 1330 us -> 967 us
  matrix products: 312 us -> 261 us
    reduce_scatter x10, waiting for transfers between devices: 971 us -> 736 us  [shard_sum(): lax.psum_scatter(term.astype(jnp.bfloat16), 'fsdp', scatter_dimension=0,...]
    psum x1 -> x0, waiting for transfers between devices: 122 us -> none  [shards(): lax.psum((gain_grad, pair_wgrad, conv_full, conv_pair_grad, bias_full, ra...]
  transfers between devices with their start and end apart: 26 -> 26, of which waited for: 20 -> 16; matrix products, arithmetic and copies ran while one was open for 14% -> 34% of each run, Pallas kernels for 0% -> 0%
where the time goes in v1:
time: 2020 us; the launch traced here: 2010 us
  waiting for transfers between devices  967 us (48%)
  local copies, waits for them, and re-layouts  331 us (16%)
  blocking collectives  293 us (15%)
  matrix products  261 us (13%)
  other arithmetic  133 us (7%)
    reduce_scatter x10, waiting for transfers between devices, shard_sum(): lax.psum_scatter(term.astype(jnp.bfloat16), 'fsdp', scatter_dimension=0,...  736 us
    dynamic_update_slice x28, local copies, waits for them, and re-layouts, span_scan(): _, outputs = lax.scan(jax.checkpoint(advance), start, items)  161 us
    all_gather x1, waiting for transfers between devices, shards(): lax.all_gather(w_down.T, 'fsdp', axis=0, tiled=True)  64.9 us
    all_gather x1, waiting for transfers between devices, shards(): lax.all_gather(w_up, 'fsdp', axis=0, tiled=True)  59.3 us
    all_gather x1, waiting for transfers between devices, shards(): lax.all_gather(w_gate, 'fsdp', axis=0, tiled=True)  58.5 us
    dot_general x12, matrix products, product(): return jnp.dot(left, right, preferred_element_type=jnp.float32)  43.6 us
    all_gather x1, blocking collectives, shards(): lax.all_gather(w_dt, 'fsdp', axis=0, tiled=True)  42.7 us
    all_gather x1, blocking collectives, shards(): lax.all_gather(w_q, 'fsdp', axis=0, tiled=True)  42.1 us
  transfers between devices with their start and end apart: 26, of which 16 were waited for; matrix products, arithmetic and copies ran while one was open for 34% of the time, Pallas kernels for 0%

profile of v1, /device:TPU:0, one launch (start us, length us, event | category | flops | bytes accessed | tf_op | source)
XLA Modules:
  0.0 2008.3 jit_solution(8543971990980998177)
XLA Ops:
  18.6 42.7 %all-gather = bf16[16,64,12]{1,2,0:T(8,128)(2,1)S(1)} all-gather(bf16[1,64,12]{1,2,0:T(8,128)(2,1)S(1)} %bitcast.715), channel_id=1, replica_groups=mesh['fsdp'=16,'tp'=2] {'fsdp'}, dimensions={0}, use_global_device_ids=true | all-gather | bytes 26112 | tf_op jit(solution)/shard_map/all_gather | solution.py:291
  62.1 37.7 %all_gather.55 = bf16[1024,64]{1,0:T(8,128)(2,1)S(1)} all-gather(bf16[64,64]{1,0:T(8,128)(2,1)S(1)} %copy-done.103), channel_id=1, replica_groups=mesh['fsdp'=16,'tp'=2] {'fsdp'}, dimensions={0}, use_global_device_ids=true | all-gather | bytes 139264 | tf_op jit(solution)/shard_map/all_gather | solution.py:293
  99.9 41.6 %all_gather.56 = bf16[1024,64]{1,0:T(8,128)(2,1)} all-gather(bf16[64,64]{1,0:T(8,128)(2,1)S(1)} %copy-done.104), channel_id=1, replica_groups=mesh['fsdp'=16,'tp'=2] {'fsdp'}, dimensions={0}, use_global_device_ids=true | all-gather | bytes 139264 | tf_op jit(solution)/shard_map/all_gather | solution.py:294
  141.4 42.1 %all_gather.51 = bf16[1024,256]{1,0:T(8,128)(2,1)} all-gather(bf16[64,256]{1,0:T(8,128)(2,1)S(1)} %copy-done.90), channel_id=1, replica_groups=mesh['fsdp'=16,'tp'=2] {'fsdp'}, dimensions={0}, use_global_device_ids=true | all-gather | bytes 557056 | tf_op jit(solution)/shard_map/all_gather | solution.py:290
  183.5 42.1 %all_gather.54 = bf16[1024,256]{1,0:T(8,128)(2,1)S(1)} all-gather(bf16[64,256]{1,0:T(8,128)(2,1)S(1)} %copy-done.91), channel_id=1, replica_groups=mesh['fsdp'=16,'tp'=2] {'fsdp'}, dimensions={0}, use_global_device_ids=true | all-gather | bytes 557056 | tf_op jit(solution)/shard_map/all_gather | solution.py:292
  225.6 40.6 %all_gather.57 = bf16[1024,256]{1,0:T(8,128)(2,1)} all-gather(bf16[64,256]{1,0:T(8,128)(2,1)S(1)} %bitcast.701), channel_id=1, replica_groups=mesh['fsdp'=16,'tp'=2] {'fsdp'}, dimensions={0}, use_global_device_ids=true | all-gather | bytes 557056 | tf_op jit(solution)/shard_map/all_gather | solution.py:295
  283.3 21.8 %while.73 = (s32[]{:T(128)}, bf16[2,512,256]{2,1,0:T(8,128)(2,1)}, f32[2,1,4,512]{3,2,1,0:T(4,128)}, s32[2,512]{1,0:T(2,128)S(1)}, s32[1024]{0:T(1024)S(1)}, /*i...) while((s32[]{:T(128)}, bf16[2,512,256]{2,1,0:T(8,128)(2,1)}, ...), condition=%wide.region_11.12_spmd.clone, body=%wide.region_8.11_spmd.clone.sunk | while | flops 563607552 | bytes 29311156 | solution.py:189
  333.5 136.9 %while.74 = (s32[]{:T(128)}, f32[12,64,128]{2,1,0:T(8,128)S(1)}, s32[]{:T(128)}, f32[4,256,12,64]{1,0,3,2:T(4,128)}, f32[4,12,64,128]{3,2,1,0:T(8,128)}, /*index...) while((s32[]{:T(128)}, f32[12,64,128]{2,1,0:T(8,128)S(1)}, ...), condition=%wide.region_6.7_spmd.clone, body=%wide.region_3.6_spmd.clone.sunk | while | flops 659144704 | bytes 10579744 | solution.py:137
  349.5 17.9 dynamic_update_slice.113
  383.6 17.9 dynamic_update_slice.113
  417.8 17.9 dynamic_update_slice.113
  451.9 17.9 dynamic_update_slice.113
  478.3 6.5 multiply_convert_fusion.2
  492.0 9.3 reduce-scatter.21.cloned.1.call-done
  507.0 59.3 %all-gather.24.cloned.1.call-done = bf16[1024,1024]{1,0:T(8,128)(2,1)} async-done(((bf16[64,1024]{1,0:T(8,128)(2,1)}), bf16[1024,1024]{1,0:T(8,128)(2,1)}) %all-gather.24.cloned.1.call-update) | async-done | bytes 2097168 | tf_op jit(solution)/shard_map/all_gather | solution.py:331
  566.4 11.5 all-gather.20.cloned.1.call-done
  577.8 6.6 fusion.235
  584.4 58.5 %all-gather.22.cloned.1.call-done = bf16[1024,1024]{1,0:T(8,128)(2,1)} async-done(((bf16[64,1024]{1,0:T(8,128)(2,1)}), bf16[1024,1024]{1,0:T(8,128)(2,1)}) %all-gather.22.cloned.1.call-update) | async-done | bytes 2097168 | tf_op jit(solution)/shard_map/all_gather | solution.py:330
  642.9 6.5 fusion.234
  653.8 64.9 %all-gather.26.cloned.1.call-done = bf16[1024,1024]{1,0:T(8,128)(2,1)} async-done(((bf16[64,1024]{1,0:T(8,128)(2,1)}), bf16[1024,1024]{1,0:T(8,128)(2,1)}) %all-gather.26.cloned.1.call-update) | async-done | bytes 2097168 | tf_op jit(solution)/shard_map/all_gather | solution.py:332
  718.7 9.8 multiply_convert_fusion
  735.5 8.4 reduce-scatter.25.cloned.1.call-done
  755.9 6.4 convolution_convert_fusion
  765.1 5.3 convolution_convert_fusion.1
  774.6 10.3 multiply_reduce_fusion.3
  787.5 5.2 reshape.810
  797.3 248.7 %while.75 = (s32[]{:T(128)}, f32[12]{0:T(128)}, f32[12,64,128]{2,1,0:T(8,128)S(1)}, f32[4,256,12,64]{1,0,3,2:T(4,128)}, f32[4,256,128]{2,1,0:T(8,128)}, /*index=...) while((s32[]{:T(128)}, f32[12]{0:T(128)}, ...), condition=%wide.region_30.31_spmd.clone, body=%wide.region_17.30_spmd.clone.sunk | while | flops 1526640640 | bytes 28226676 | solution.py:137
  841.3 17.9 dynamic_update_slice.117
  903.5 17.9 dynamic_update_slice.117
  965.8 17.9 dynamic_update_slice.117
  1028.1 17.9 dynamic_update_slice.117
  1046.0 50.8 %while.76 = (s32[]{:T(128)}, f32[1024,1,64]{0,2,1:T(8,128)}, f32[1024,1,64]{0,2,1:T(8,128)}, f32[2,512,256]{1,0,2:T(2,128)}, bf16[2,512,1,4,64]{1,4,3,2,0:T(8,12...) while((s32[]{:T(128)}, f32[1024,1,64]{0,2,1:T(8,128)}, ...), condition=%wide.region_33.34_spmd.clone, body=%wide.region_31.33_spmd.clone.sunk | while | flops 1375664128 | bytes 77013336 | solution.py:243
  1061.1 10.3 dynamic_update_slice.119
  1086.1 10.3 dynamic_update_slice.119
  1138.7 6.3 multiply_reduce_fusion.7
  1151.9 5.2 convolution_convert_fusion.3
  1169.8 7.9 add_convert_fusion
  1177.8 5.4 convolution_convert_fusion.2
  1192.9 66.7 %reduce-scatter.37.cloned.1.call-done = bf16[64,64]{1,0:T(8,128)(2,1)} async-done(((bf16[1024,64]{1,0:T(8,128)(2,1)}), bf16[64,64]{1,0:T(8,128)(2,1)}) %reduce-scatter.37.cloned.1.call-update) | async-done | bytes 8208 | tf_op jit(solution)/shard_map/reduce_scatter | solution.py:48
  1260.9 73.2 %reduce-scatter.39.cloned.1.call-done = bf16[64,64]{1,0:T(8,128)(2,1)} async-done(((bf16[1024,64]{1,0:T(8,128)(2,1)}), bf16[64,64]{1,0:T(8,128)(2,1)}) %reduce-scatter.39.cloned.1.call-update) | async-done | bytes 8208 | tf_op jit(solution)/shard_map/reduce_scatter | solution.py:48
  1335.5 73.9 %reduce-scatter.35.cloned.1.call-done = bf16[64,256]{1,0:T(8,128)(2,1)} async-done(((bf16[1024,256]{1,0:T(8,128)(2,1)}), bf16[64,256]{1,0:T(8,128)(2,1)}) %reduce-scatter.35.cloned.1.call-update) | async-done | bytes 32784 | tf_op jit(solution)/shard_map/reduce_scatter | solution.py:48
  1410.8 74.2 %reduce-scatter.33.cloned.1.call-done = bf16[64,256]{1,0:T(8,128)(2,1)} async-done(((bf16[1024,256]{1,0:T(8,128)(2,1)}), bf16[64,256]{1,0:T(8,128)(2,1)}) %reduce-scatter.33.cloned.1.call-update) | async-done | bytes 32784 | tf_op jit(solution)/shard_map/reduce_scatter | solution.py:48
  1489.7 70.5 %reduce-scatter.41.cloned.1.call-done = bf16[64,256]{1,0:T(8,128)(2,1)} async-done(((bf16[1024,256]{1,0:T(8,128)(2,1)}), bf16[64,256]{1,0:T(8,128)(2,1)}) %reduce-scatter.41.cloned.1.call-update) | async-done | bytes 32784 | tf_op jit(solution)/shard_map/reduce_scatter | solution.py:48
  1561.6 124.4 %reduce-scatter.29.cloned.1.call-done = bf16[64,768]{1,0:T(8,128)(2,1)} async-done(((bf16[1024,768]{1,0:T(8,128)(2,1)}), bf16[64,768]{1,0:T(8,128)(2,1)}) %reduce-scatter.29.cloned.1.call-update) | async-done | bytes 98320 | tf_op jit(solution)/shard_map/reduce_scatter | solution.py:48
  1687.6 126.8 %reduce-scatter.31.cloned.1.call-done = bf16[64,768]{1,0:T(8,128)(2,1)} async-done(((bf16[1024,768]{1,0:T(8,128)(2,1)}), bf16[64,768]{1,0:T(8,128)(2,1)}) %reduce-scatter.31.cloned.1.call-update) | async-done | bytes 98320 | tf_op jit(solution)/shard_map/reduce_scatter | solution.py:48
  1816.0 126.6 %reduce-scatter.43.cloned.1.call-done = bf16[64,768]{1,0:T(8,128)(2,1)} async-done(((bf16[1024,768]{1,0:T(8,128)(2,1)}), bf16[64,768]{1,0:T(8,128)(2,1)}) %reduce-scatter.43.cloned.1.call-update) | async-done | bytes 98320 | tf_op jit(solution)/shard_map/reduce_scatter | solution.py:48
  1944.2 9.3 reduce-scatter.27.cloned.1.call-done
  1955.7 41.8 %all-reduce.30 = (f32[1024]{0:T(1024)}, f32[4,1536]{1,0:T(4,128)}, f32[4,256]{1,0:T(4,128)}, f32[24]{0:T(128)}, f32[24]{0:T(128)}, /*index=5*/f32[24]{0:T(128)}, f32[1024]{0:T(1024)}) all-reduce(f32[1024]{0:T(1024)S(1)} %get-tuple-element.1132, ...), channel_id=1, replica_groups=mesh['fsdp'=16,'tp'=2] {'fsdp','tp'}, use_global_device_ids=true, to_apply=%region_37.38 | all-reduce | flops 9288 | bytes 74304 | tf_op jit(solution)/shard_map/psum | solution.py:455
  (897 shorter events, 495.8 us)
Async XLA Ops:
  7.3 92.6 %copy-start.104 = (bf16[64,64]{1,0:T(8,128)(2,1)S(1)}, bf16[64,64]{1,0:T(8,128)(2,1)}, u32[]{:S(2)}) copy-start(bf16[64,64]{1,0:T(8,128)(2,1)} %param.45) | copy-start | bytes 24580
  7.3 134.1 %copy-start.90 = (bf16[64,256]{1,0:T(8,128)(2,1)S(1)}, bf16[64,256]{1,0:T(8,128)(2,1)}, u32[]{:S(2)}) copy-start(bf16[64,256]{1,0:T(8,128)(2,1)} %param.36) | copy-start | bytes 98308
  7.3 176.2 %copy-start.91 = (bf16[64,256]{1,0:T(8,128)(2,1)S(1)}, bf16[64,256]{1,0:T(8,128)(2,1)}, u32[]{:S(2)}) copy-start(bf16[64,256]{1,0:T(8,128)(2,1)} %param.43) | copy-start | bytes 98308
  7.3 218.3 %copy-start.92 = (bf16[256,64]{0,1:T(8,128)(2,1)S(1)}, bf16[256,64]{0,1:T(8,128)(2,1)}, u32[]{:S(2)}) copy-start(bf16[256,64]{0,1:T(8,128)(2,1)} %param.46) | copy-start | bytes 98308
  7.3 260.9 %all-gather.12.cloned.1.call-start = ((), (), s32[]{:S(2)}) async-start(), calls=%async_computation.16 | async-start | bytes 3145728 | tf_op jit(solution)/shard_map/all_gather | solution.py:299
  10.0 257.5 %copy-start.114 = (f32[4,1536]{1,0:T(4,128)S(1)}, f32[4,1536]{1,0:T(4,128)}, u32[]{:S(2)}) copy-start(f32[4,1536]{1,0:T(4,128)} %param.38) | copy-start | bytes 73732
  12.5 298.0 %all-gather.14.cloned.1.call-start = ((), (), s32[]{:S(2)}) async-start(), calls=%async_computation.17 | async-start | bytes 1671168 | tf_op jit(solution)/shard_map/all_gather | solution.py:289
  13.3 465.0 %all-gather.16.cloned.1.call-start = ((), (), s32[]{:S(2)}) async-start(), calls=%async_computation.18 | async-start | bytes 1671168 | tf_op jit(solution)/shard_map/all_gather | solution.py:288
  14.0 470.8 %all-gather.18.cloned.1.call-start = ((), (), s32[]{:S(2)}) async-start(), calls=%async_computation.19 | async-start | bytes 1671168 | tf_op jit(solution)/shard_map/all_gather | solution.py:296
  14.6 486.8 %reduce-scatter.21.cloned.1.call-start = ((), (), s32[]{:S(2)}) async-start(), calls=%async_computation.20 | async-start | bytes 6291456 | tf_op jit(solution)/shard_map/reduce_scatter | solution.py:325
  14.7 253.5 %copy-start.115 = (f32[32]{0:T(128)}, f32[32]{0:T(128)S(1)}, u32[]{:S(2)}) copy-start(f32[32]{0:T(128)S(1)} %multiply_power_fusion) | copy-start | bytes 388
  17.2 745.2 %copy-start.62 = (f32[1024]{0:T(1024)}, f32[1024]{0:T(1024)S(1)}, u32[]{:S(2)}) copy-start(f32[1024]{0:T(1024)S(1)} %pad_convert_fusion.1) | copy-start | bytes 12292
  17.3 250.9 %copy-start.74 = (f32[1024]{0:T(1024)}, f32[1024]{0:T(1024)S(1)}, u32[]{:S(2)}) copy-start(f32[1024]{0:T(1024)S(1)} %subtract_convert_fusion.1) | copy-start | bytes 12292
  99.9 176.7 %copy-start.35 = (bf16[1024,64]{1,0:T(8,128)(2,1)}, bf16[1024,64]{1,0:T(8,128)(2,1)S(1)}, u32[]{:S(2)}) copy-start(bf16[1024,64]{1,0:T(8,128)(2,1)S(1)} %all_gather.55) | copy-start | bytes 393220
  491.4 75.0 %all-gather.24.cloned.1.call-start = ((), (), s32[]{:S(2)}) async-start(), calls=%async_computation.23 | async-start | bytes 2228224 | tf_op jit(solution)/shard_map/all_gather | solution.py:331
  492.0 85.9 %all-gather.20.cloned.1.call-start = ((), (), s32[]{:S(2)}) async-start(), calls=%async_computation.21 | async-start | bytes 3145728 | tf_op jit(solution)/shard_map/all_gather | solution.py:328
  503.3 243.1 %copy-start.7 = (f32[512,1024]{1,0:T(8,128)}, f32[512,1024]{1,0:T(8,128)S(1)}, u32[]{:S(2)}) copy-start(f32[512,1024]{1,0:T(8,128)S(1)} %get-tuple-element.1256) | copy-start | bytes 6291460
  503.3 243.1 %copy-start.76 = (f32[512]{0:T(512)}, f32[512]{0:T(512)S(1)}, u32[]{:S(2)}) copy-start(f32[512]{0:T(512)S(1)} %fusion.216) | copy-start | bytes 6148
  504.7 138.1 %all-gather.22.cloned.1.call-start = ((), (), s32[]{:S(2)}) async-start(), calls=%async_computation.22 | async-start | bytes 2228224 | tf_op jit(solution)/shard_map/all_gather | solution.py:330
  505.5 148.3 %all-gather.28.cloned.1.call-start = ((), (), s32[]{:S(2)}) async-start(), calls=%async_computation.26 | async-start | bytes 3145728 | tf_op jit(solution)/shard_map/all_gather | solution.py:345
  506.2 212.4 %all-gather.26.cloned.1.call-start = ((), (), s32[]{:S(2)}) async-start(), calls=%async_computation.24 | async-start | bytes 2228224 | tf_op jit(solution)/shard_map/all_gather | solution.py:332
  506.8 237.0 %reduce-scatter.25.cloned.1.call-start = ((), (), s32[]{:S(2)}) async-start(), calls=%async_computation.27 | async-start | bytes 3145728 | tf_op jit(solution)/shard_map/reduce_scatter | solution.py:358
  735.4 35.1 %all-gather.30.cloned.1.call-start = ((), (), s32[]{:S(2)}) async-start(), calls=%async_computation.28 | async-start | bytes 3145728 | tf_op jit(solution)/shard_map/all_gather | solution.py:363
  748.1 435.1 %reduce-scatter.51.cloned.1.call-start = ((), (), s32[]{:S(2)}) async-start(), calls=%async_computation.41 | async-start | bytes 2228224
  755.9 431.4 %reduce-scatter.47.cloned.1.call-start = ((), (), s32[]{:S(2)}) async-start(), calls=%async_computation.39 | async-start | bytes 2228224 | tf_op jit(solution)/shard_map/reduce_scatter | solution.py:48
  762.4 426.6 %reduce-scatter.45.cloned.1.call-start = ((), (), s32[]{:S(2)}) async-start(), calls=%async_computation.38 | async-start | bytes 2228224 | tf_op jit(solution)/shard_map/reduce_scatter | solution.py:48
  770.4 421.1 %reduce-scatter.49.cloned.1.call-start = ((), (), s32[]{:S(2)}) async-start(), calls=%async_computation.40 | async-start | bytes 278528
  797.3 248.8 %copy-start.12 = (bf16[2,512,1,4,64]{1,4,3,2,0:T(8,128)(2,1)S(1)}, bf16[2,512,1,4,64]{1,4,3,2,0:T(8,128)(2,1)}, u32[]{:S(2)}) copy-start(bf16[2,512,1,4,64]{1,4,3,2,0:T(8,128)(2,1)} %copy-done.11) | copy-start | bytes 1572868
  797.3 248.8 %copy-start.14 = (bf16[1024,1,64]{0,2,1:T(8,128)(2,1)S(1)}, bf16[1024,1,64]{0,2,1:T(8,128)(2,1)}, u32[]{:S(2)}) copy-start(bf16[1024,1,64]{0,2,1:T(8,128)(2,1)} %copy-done.13) | copy-start | bytes 393220
  1107.5 152.1 %reduce-scatter.37.cloned.1.call-start = ((), (), s32[]{:S(2)}) async-start(), calls=%async_computation.34 | async-start | bytes 278528 | tf_op jit(solution)/shard_map/reduce_scatter | solution.py:48
  1111.0 223.2 %reduce-scatter.39.cloned.1.call-start = ((), (), s32[]{:S(2)}) async-start(), calls=%async_computation.35 | async-start | bytes 278528 | tf_op jit(solution)/shard_map/reduce_scatter | solution.py:48
  1112.5 296.9 %reduce-scatter.35.cloned.1.call-start = ((), (), s32[]{:S(2)}) async-start(), calls=%async_computation.33 | async-start | bytes 557056 | tf_op jit(solution)/shard_map/reduce_scatter | solution.py:48
  1115.3 369.7 %reduce-scatter.33.cloned.1.call-start = ((), (), s32[]{:S(2)}) async-start(), calls=%async_computation.32 | async-start | bytes 557056 | tf_op jit(solution)/shard_map/reduce_scatter | solution.py:48
  1122.8 437.5 %reduce-scatter.41.cloned.1.call-start = ((), (), s32[]{:S(2)}) async-start(), calls=%async_computation.36 | async-start | bytes 557056 | tf_op jit(solution)/shard_map/reduce_scatter | solution.py:48
  1126.0 560.0 %reduce-scatter.29.cloned.1.call-start = ((), (), s32[]{:S(2)}) async-start(), calls=%async_computation.30 | async-start | bytes 1671168 | tf_op jit(solution)/shard_map/reduce_scatter | solution.py:48
  1130.5 683.9 %reduce-scatter.31.cloned.1.call-start = ((), (), s32[]{:S(2)}) async-start(), calls=%async_computation.31 | async-start | bytes 1671168 | tf_op jit(solution)/shard_map/reduce_scatter | solution.py:48
  1151.8 790.8 %reduce-scatter.43.cloned.1.call-start = ((), (), s32[]{:S(2)}) async-start(), calls=%async_computation.37 | async-start | bytes 1671168 | tf_op jit(solution)/shard_map/reduce_scatter | solution.py:48
  1157.1 796.4 %reduce-scatter.27.cloned.1.call-start = ((), (), s32[]{:S(2)}) async-start(), calls=%async_computation.29 | async-start | bytes 3145728 | tf_op jit(solution)/shard_map/reduce_scatter | solution.py:404
  1177.7 819.8 %reduce-scatter.23.cloned.1.call-start = ((), (), s32[]{:S(2)}) async-start(), calls=%async_computation.25 | async-start | bytes 3145728 | tf_op jit(solution)/shard_map/reduce_scatter | solution.py:338
  1183.2 770.3 %copy-start.10 = (bf16[512,1024]{1,0:T(8,128)(2,1)S(1)}, bf16[512,1024]{1,0:T(8,128)(2,1)}, u32[]{:S(2)}) copy-start(bf16[512,1024]{1,0:T(8,128)(2,1)} %param.30) | copy-start | bytes 3145732
  1183.2 770.3 %copy-start.78 = (f32[1024]{0:T(1024)S(1)}, f32[1024]{0:T(1024)}, u32[]{:S(2)}) copy-start(f32[1024]{0:T(1024)} %param.33) | copy-start | bytes 12292
  1183.2 770.3 %copy-start.94 = (f32[512]{0:T(512)S(1)}, f32[512]{0:T(512)}, u32[]{:S(2)}) copy-start(f32[512]{0:T(512)} %copy-done.93) | copy-start | bytes 6148
  1183.2 772.5 %copy-start.102 = (f32[1024]{0:T(1024)S(1)}, f32[1024]{0:T(1024)}, u32[]{:S(2)}) copy-start(f32[1024]{0:T(1024)} %get-tuple-element.1126) | copy-start | bytes 12292
  1183.2 814.2 %copy-start.98 = (f32[512]{0:T(512)S(1)}, f32[512]{0:T(512)}, u32[]{:S(2)}) copy-start(f32[512]{0:T(512)} %copy-done.97) | copy-start | bytes 6148
  1183.2 814.3 %copy-start.8 = (f32[512,1024]{1,0:T(8,128)S(1)}, f32[512,1024]{1,0:T(8,128)}, u32[]{:S(2)}) copy-start(f32[512,1024]{1,0:T(8,128)} %copy-done.7) | copy-start | bytes 6291460
  1183.2 814.3 %copy-start.73 = (f32[1024]{0:T(1024)S(1)}, f32[1024]{0:T(1024)}, u32[]{:S(2)}) copy-start(f32[1024]{0:T(1024)} %param.48) | copy-start | bytes 12292
  1183.2 814.3 %copy-start.77 = (f32[512]{0:T(512)S(1)}, f32[512]{0:T(512)}, u32[]{:S(2)}) copy-start(f32[512]{0:T(512)} %copy-done.76) | copy-start | bytes 6148
  1183.3 814.3 %copy-start.96 = (f32[512]{0:T(512)S(1)}, f32[512]{0:T(512)}, u32[]{:S(2)}) copy-start(f32[512]{0:T(512)} %copy-done.95) | copy-start | bytes 6148
  (142 other events, 831.8 us)
Sparse Core Ops, SparseCore 0:
  12.7 13.2 all-gather.11
  28.7 60.0 all-gather.13
  91.6 59.9 all-gather.15
  154.2 59.2 all-gather.17
  491.5 9.8 reduce-scatter.20
  504.4 61.9 all-gather.23
  568.6 9.2 all-gather.19
  581.0 61.8 all-gather.21
  644.5 9.2 all-gather.27
  656.8 61.8 all-gather.25
  735.5 8.2 reduce-scatter.24
  748.3 11.7 all-gather.29
  762.3 81.7 reduce-scatter.50
  846.3 78.0 reduce-scatter.46
  926.5 77.3 reduce-scatter.44
  1107.6 77.3 reduce-scatter.48
  1187.2 72.4 reduce-scatter.36
  1261.7 72.4 reduce-scatter.38
  1336.5 72.8 reduce-scatter.34
  1412.0 72.8 reduce-scatter.32
  1487.3 72.8 reduce-scatter.40
  1565.0 120.9 reduce-scatter.28
  1690.8 123.5 reduce-scatter.30
  1819.1 123.5 reduce-scatter.42
  1944.9 8.5 reduce-scatter.26
  1955.7 10.7 reduce-scatter.22
